TPU v7x, 512 devices: a whole 4x8x8 slice. The times are simulated.
512 devices in a mesh: seq: 64 (over y, x, core), tp: 8 (over z).
Axes of the slice: x: 4, y: 8, z: 8, core: 2. Of those that a mesh axis runs over, the one named last changes fastest.
Arguments:
- queries: bfloat16 [32768, 4096], P('seq', 'tp'), may hold values from -9 to 9
- keys: bfloat16 [32768, 4096], P('seq', 'tp'), may hold values from -9 to 9
- values: bfloat16 [32768, 4096], P('seq', 'tp'), may hold values from -6 to 6
- route: int32 [32, 32768], P('tp', 'seq'), may hold values from 0 to 32767, as said below
- members: int32 [32, 32768], P('tp', 'seq'), may hold values from 0 to 32767, as said below
- pattern: int32 [32, 128, 10], P('tp', 'seq'), may hold values from 0 to 1, as said below
- w_out: bfloat16 [4096, 4096], P('tp', 'seq'), may hold values from -0.25 to 0.25
Outputs:
- mixed: bfloat16 [32768, 4096], P('seq', 'tp')
Inputs may be any that keep to these rules, and one draw needn't show every extreme that they name: `route`: each row is a permutation of the positions; for every aligned block of 512 positions and every aligned block of 512 slots, exactly 8 of the block's positions have their slot in that slot block. members[h] is the inverse permutation of route[h]: members[h, route[h, p]] = p. `pattern`: entries 2 * 2 and 2 * 2 + 1 (the cluster's own blocks) are always 1; entries whose cluster lies outside 0 to 127 are always 0.
All inputs are finite; a program needn't handle non-finite values.
Results may differ from a plain program's by a relative error of at most 0.017.
Values may be sent and summed in bfloat16 or wider, within the bound.
A program may use at most 64 MiB of HBM per device.

v0:
```python
import jax
import jax.numpy as jnp
from jax import lax
from jax.sharding import PartitionSpec as P

CLUSTER = 256
REACH = 2


def extended_2(cells, sides, width):
    for axis, dim in sides:
        count = lax.axis_size(axis)
        ends = count - 1
        head = lax.slice_in_dim(cells, 0, width, axis=dim)
        tail = lax.slice_in_dim(cells, cells.shape[dim] - width, cells.shape[dim], axis=dim)
        cells = jnp.concatenate(
            [
                lax.ppermute(tail, axis, [(i, (i + 1) % count) for i in range(ends)]),
                cells,
                lax.ppermute(head, axis, [((i + 1) % count, i) for i in range(ends)]),
            ],
            axis=dim,
        )
    return cells


def attend_head(pieces):
    query_rows, key_rows, value_rows, pattern_rows = pieces
    head_width = query_rows.shape[1]
    cluster_count = query_rows.shape[0] // CLUSTER
    window_rows = (2 * REACH + 1) * CLUSTER
    starts = jnp.arange(cluster_count) * CLUSTER
    key_window = jax.vmap(
        lambda slot_start: lax.dynamic_slice_in_dim(key_rows, slot_start, window_rows, 0)
    )(starts)
    value_window = jax.vmap(
        lambda slot_start: lax.dynamic_slice_in_dim(value_rows, slot_start, window_rows, 0)
    )(starts)
    query_blocks = query_rows.reshape(cluster_count, CLUSTER, head_width)
    scores = jnp.einsum(
        "cqd,ckd->cqk", query_blocks, key_window, preferred_element_type=jnp.float32
    ) * head_width ** (-0.5)
    allowed = jnp.repeat(pattern_rows, CLUSTER // 2, axis=1) > 0
    scores = jnp.where(allowed[:, None, :], scores, -jnp.inf)
    row_max = jnp.max(scores, axis=-1, keepdims=True)
    exponent = jnp.exp(scores - row_max)
    weights = (exponent / jnp.sum(exponent, axis=-1, keepdims=True)).astype(jnp.bfloat16)
    context = jnp.einsum(
        "cqk,ckd->cqd", weights, value_window, preferred_element_type=jnp.float32
    ).astype(jnp.bfloat16)
    return context.reshape(query_rows.shape[0], head_width)


def buffer_index(group_of, order_key, per_peer):
    same_group = group_of[:, :, None] == group_of[:, None, :]
    earlier = order_key[:, None, :] < order_key[:, :, None]
    rank = jnp.sum((same_group & earlier).astype(jnp.int32), axis=2)
    return group_of * per_peer + rank


def shards(queries, keys, values, route, members, pattern, w_out):
    rows_here = queries.shape[0]
    head_count = route.shape[0]
    head_width = queries.shape[1] // head_count
    peer_count = lax.axis_size("seq")
    per_peer = rows_here // peer_count
    local_iota = jnp.arange(rows_here, dtype=jnp.int32)
    send_index = buffer_index(route // rows_here, route, per_peer)
    local_slots = jnp.broadcast_to(local_iota[None, :], members.shape)
    arrival_index = buffer_index(members // rows_here, local_slots, per_peer)
    send_table = (send_index[:, None, :] == local_iota[None, :, None]).astype(jnp.bfloat16)
    land_table = (arrival_index[:, :, None] == local_iota[None, None, :]).astype(jnp.bfloat16)
    stacked = jnp.concatenate(
        [
            queries.reshape(rows_here, head_count, head_width),
            keys.reshape(rows_here, head_count, head_width),
            values.reshape(rows_here, head_count, head_width),
        ],
        axis=2,
    )
    packed = jnp.einsum(
        "hap,phd->had", send_table, stacked, preferred_element_type=jnp.float32
    ).astype(jnp.bfloat16)

    def outgoing(column_index):
        part_rows = packed[:, :, column_index * head_width : (column_index + 1) * head_width]
        return part_rows.reshape(head_count, peer_count, per_peer, head_width)

    sent_query, sent_key, sent_value = (
        lax.all_to_all(outgoing(0), "seq", split_axis=1, concat_axis=1, tiled=True),
        lax.all_to_all(outgoing(1), "seq", split_axis=1, concat_axis=1, tiled=True),
        lax.all_to_all(outgoing(2), "seq", split_axis=1, concat_axis=1, tiled=True),
    )
    arrived = jnp.concatenate(
        [
            sent_query.reshape(head_count, rows_here, head_width),
            sent_key.reshape(head_count, rows_here, head_width),
            sent_value.reshape(head_count, rows_here, head_width),
        ],
        axis=2,
    )
    placed = jnp.einsum(
        "hsa,had->hsd", land_table, arrived, preferred_element_type=jnp.float32
    ).astype(jnp.bfloat16)
    ordered_query = placed[:, :, :head_width]
    keys_values = jnp.stack(
        [placed[:, :, head_width : 2 * head_width], placed[:, :, 2 * head_width :]]
    )
    extended = extended_2(keys_values, (("seq", 2),), REACH * CLUSTER)
    context = lax.map(attend_head, (ordered_query, extended[0], extended[1], pattern))
    returning = jnp.einsum(
        "hsa,hsd->had", land_table, context, preferred_element_type=jnp.float32
    ).astype(jnp.bfloat16)
    returning = returning.reshape(head_count, peer_count, per_peer, head_width)
    returned = lax.all_to_all(returning, "seq", split_axis=1, concat_axis=1, tiled=True).reshape(
        head_count, rows_here, head_width
    )
    attended = jnp.einsum(
        "hap,had->phd", send_table, returned, preferred_element_type=jnp.float32
    ).astype(jnp.bfloat16)
    attended = attended.reshape(rows_here, head_count * head_width)
    partial_value = jnp.dot(
        attended,
        lax.all_gather(w_out, "seq", axis=1, tiled=True),
        preferred_element_type=jnp.float32,
    )
    column_count = partial_value.shape[1] // lax.axis_size("tp")
    summed = lax.psum(partial_value.astype(jnp.bfloat16), "tp").astype(jnp.float32)
    mixed_out = lax.dynamic_slice_in_dim(
        summed, lax.axis_index("tp") * column_count, column_count, 1
    )
    return mixed_out.astype(jnp.bfloat16)


def solution(mesh):
    placed = (
        P("seq", "tp"),
        P("seq", "tp"),
        P("seq", "tp"),
        P("tp", "seq"),
        P("tp", "seq"),
        P("tp", "seq", None),
        P("tp", "seq"),
    )
    return jax.shard_map(
        shards, mesh=mesh, in_specs=placed, out_specs=P("seq", "tp"), check_vma=False
    )
```

profile of v0, /device:TPU:1, one launch (start us, length us, event | category | flops | bytes accessed | tf_op | source)
XLA Modules:
  0.0 320.6 jit_solution(11738363935786757012)
XLA Ops:
  6.5 0.8 add_select_fusion
  7.3 1.8 convert_reduce_fusion
  9.1 0.7 multiply_add_fusion
  9.9 1.3 copy.34
  11.4 1.3 copy.35
  13.4 1.3 fusion.22
  15.1 0.9 copy.44
  16.0 11.6 %all-to-all-start.2 = ((bf16[4,64,8,128]{3,2,0,1:T(8,128)(2,1)}), bf16[4,64,8,128]{3,2,0,1:T(8,128)(2,1)S(1)}, u32[]{:S(2)}, u32[]{:S(2)}) async-start(bf16[4,64,8,128]{3,2,0,1:T(8,128)(2,1)} %copy.44), calls=%async_computation.2 | async-start | bytes 1048576 | tf_op jit(solution)/shard_map/all_to_all | solution.py:92
  27.6 0.9 copy.42
  28.5 16.8 %all-to-all-done.2 = bf16[4,64,8,128]{3,2,0,1:T(8,128)(2,1)S(1)} async-done(((bf16[4,64,8,128]{3,2,0,1:T(8,128)(2,1)}), bf16[4,64,8,128]{3,2,0,1:T(8,128)(2,1)S(1)}, u32[]{:S(2)}, u32[]{:S(2)}) %all-to-all-start.2) | async-done | bytes 524320 | tf_op jit(solution)/shard_map/all_to_all | solution.py:92
  45.3 5.7 %all-to-all-start.1 = ((bf16[4,64,8,128]{3,2,0,1:T(8,128)(2,1)}), bf16[4,64,8,128]{3,2,0,1:T(8,128)(2,1)S(1)}, u32[]{:S(2)}, u32[]{:S(2)}) async-start(bf16[4,64,8,128]{3,2,0,1:T(8,128)(2,1)} %copy.42), calls=%async_computation.1 | async-start | bytes 1048576 | tf_op jit(solution)/shard_map/all_to_all | solution.py:91
  51.0 0.9 copy.40
  51.9 16.8 %all-to-all-done.1 = bf16[4,64,8,128]{3,2,0,1:T(8,128)(2,1)S(1)} async-done(((bf16[4,64,8,128]{3,2,0,1:T(8,128)(2,1)}), bf16[4,64,8,128]{3,2,0,1:T(8,128)(2,1)S(1)}, u32[]{:S(2)}, u32[]{:S(2)}) %all-to-all-start.1) | async-done | bytes 524320 | tf_op jit(solution)/shard_map/all_to_all | solution.py:91
  68.8 5.7 %all-to-all-start = ((bf16[4,64,8,128]{3,2,0,1:T(8,128)(2,1)}), bf16[4,64,8,128]{3,2,0,1:T(8,128)(2,1)S(1)}, u32[]{:S(2)}, u32[]{:S(2)}) async-start(bf16[4,64,8,128]{3,2,0,1:T(8,128)(2,1)} %copy.40), calls=%async_computation | async-start | bytes 1048576 | tf_op jit(solution)/shard_map/all_to_all | solution.py:90
  74.7 1.2 convert_reduce_fusion.1
  76.1 16.1 %all-to-all-done = bf16[4,64,8,128]{3,2,0,1:T(8,128)(2,1)S(1)} async-done(((bf16[4,64,8,128]{3,2,0,1:T(8,128)(2,1)}), bf16[4,64,8,128]{3,2,0,1:T(8,128)(2,1)S(1)}, u32[]{:S(2)}, u32[]{:S(2)}) %all-to-all-start) | async-done | bytes 524320 | tf_op jit(solution)/shard_map/all_to_all | solution.py:90
  92.3 1.3 fusion.21
  93.6 1.2 slice_bitcast_fusion.3
  94.9 3.4 %collective-permute-start = (bf16[2,4,512,128]{3,2,1,0:T(8,128)(2,1)S(1)}, bf16[2,4,512,128]{3,2,1,0:T(8,128)(2,1)S(1)}, u32[]{:S(2)}, u32[]{:S(2)}) collective-permute-start(bf16[2,4,512,128]{3,2,1,0:T(8,128)(2,1)S(1)} %pad_maximum_fusion.1), channel_id=1, source_target_pairs={{0,8},{8,16},{16,24},{24,32},{32,40},{40,48},{48,56},{56,64},{64,7... | collective-permute-start | bytes 3145736 | tf_op jit(solution)/shard_map/ppermute | solution.py:18
  98.3 1.9 collective-permute-start.1
  100.5 9.5 %collective-permute-done = bf16[2,4,512,128]{3,2,1,0:T(8,128)(2,1)S(1)} collective-permute-done((bf16[2,4,512,128]{3,2,1,0:T(8,128)(2,1)S(1)}, bf16[2,4,512,128]{3,2,1,0:T(8,128)(2,1)S(1)}, u32[]{:S(2)}, u32[]{:S(2)}) %collective-permute-start) | collective-permute-done | bytes 1048608 | tf_op jit(solution)/shard_map/ppermute | solution.py:18
  110.0 4.5 %collective-permute-done.1 = bf16[2,4,512,128]{3,2,1,0:T(8,128)(2,1)} collective-permute-done((bf16[2,4,512,128]{3,2,1,0:T(8,128)(2,1)S(1)}, bf16[2,4,512,128]{3,2,1,0:T(8,128)(2,1)}, u32[]{:S(2)}, u32[]{:S(2)}) %collective-permute-start.1) | collective-permute-done | bytes 1048608 | tf_op jit(solution)/shard_map/ppermute | solution.py:20
  114.5 1.3 pad_maximum_fusion
  115.8 1.4 slice_bitcast_fusion
  117.2 27.3 %while.16 = (s32[]{:T(128)}, bf16[4,512,128]{2,1,0:T(8,128)(2,1)}, s32[4,2,10]{2,1,0:T(2,128)}, bf16[4,512,128]{2,1,0:T(8,128)(2,1)}, bf16[4,1536,128]{2,1,0:T(8...) while((s32[]{:T(128)}, bf16[4,512,128]{2,1,0:T(8,128)(2,1)}, ...), condition=%wide.region_5.6_spmd, body=%wide.region_2.5_spmd.sunk | while | flops 509283360 | bytes 7096867 | solution.py:110
  117.2 1.1 dynamic-slice_bitcast_fusion.3
  118.8 0.9 constant_dynamic-slice_fusion.7
  120.5 1.0 fusion.65
  122.0 1.4 fusion.66
  124.0 1.0 dynamic-slice_bitcast_fusion.3
  125.6 0.9 constant_dynamic-slice_fusion.7
  127.3 1.0 fusion.65
  128.8 1.4 fusion.66
  130.9 1.0 dynamic-slice_bitcast_fusion.3
  132.4 0.9 constant_dynamic-slice_fusion.7
  134.1 1.0 fusion.65
  135.6 1.4 fusion.66
  137.7 1.1 dynamic-slice_bitcast_fusion.3
  139.3 0.9 constant_dynamic-slice_fusion.7
  141.0 1.0 fusion.65
  142.4 1.4 fusion.66
  144.5 1.8 fusion.35
  146.5 31.2 %all_to_all.20 = bf16[4,64,8,128]{3,2,0,1:T(8,128)(2,1)S(1)} all-to-all(bf16[4,64,8,128]{3,2,0,1:T(8,128)(2,1)S(1)} %copy.47), channel_id=1, replica_groups=mesh['seq'=64,'tp'=8] {'seq'}, dimensions={1} | all-to-all | bytes 1048576 | tf_op jit(solution)/shard_map/all_to_all | solution.py:115
  177.6 0.9 fusion.34
  178.6 11.8 %all-gather.2.cloned.1.call-done = bf16[512,4096]{0,1:T(8,128)(2,1)} async-done(((bf16[512,64]{0,1:T(8,128)(2,1)}), bf16[512,4096]{0,1:T(8,128)(2,1)}) %all-gather.2.cloned.1.call-update) | async-done | bytes 4194320 | tf_op jit(solution)/shard_map/all_gather | solution.py:124
  190.3 6.6 %convolution_convert_fusion = bf16[512,4096]{1,0:T(8,128)(2,1)} fusion(bf16[512,512]{0,1:T(8,128)(2,1)S(1)} %bitcast.112, bf16[512,4096]{0,1:T(8,128)(2,1)} %all-gather.2.cloned.1.call-done), kind=kOutput, calls=%fused_computation.26 | convolution fusion | flops 2149580800 | bytes 8912896 | tf_op jit(solution)/shard_map/dot_general | solution.py:122
  196.9 115.0 %all-reduce.3.cloned.1.call-done = bf16[512,4096]{1,0:T(8,128)(2,1)} async-done(((bf16[512,4096]{1,0:T(8,128)(2,1)}), bf16[512,4096]{1,0:T(8,128)(2,1)}) %all-reduce.3.cloned.1.call-update) | async-done | bytes 4194320 | tf_op jit(solution)/shard_map/psum | solution.py:128
  311.9 1.9 convert_convert_fusion
  (94 shorter events, 14.7 us)
Async XLA Ops:
  6.5 6.4 %copy-start = (bf16[512,512]{1,0:T(8,128)(2,1)S(1)}, bf16[512,512]{1,0:T(8,128)(2,1)}, u32[]{:S(2)}) copy-start(bf16[512,512]{1,0:T(8,128)(2,1)} %param.11) | copy-start | bytes 1572868
  15.1 59.6 %copy-start.1 = (s32[4,512]{1,0:T(4,128)S(1)}, s32[4,512]{1,0:T(4,128)}, u32[]{:S(2)}) copy-start(s32[4,512]{1,0:T(4,128)} %param.13) | copy-start | bytes 24580
  16.0 29.3 %all-to-all-start.2 = ((bf16[4,64,8,128]{3,2,0,1:T(8,128)(2,1)}), bf16[4,64,8,128]{3,2,0,1:T(8,128)(2,1)S(1)}, u32[]{:S(2)}, u32[]{:S(2)}) async-start(bf16[4,64,8,128]{3,2,0,1:T(8,128)(2,1)} %copy.44), calls=%async_computation.2 | async-start | bytes 1048576 | tf_op jit(solution)/shard_map/all_to_all | solution.py:92
  45.3 23.4 %all-to-all-start.1 = ((bf16[4,64,8,128]{3,2,0,1:T(8,128)(2,1)}), bf16[4,64,8,128]{3,2,0,1:T(8,128)(2,1)S(1)}, u32[]{:S(2)}, u32[]{:S(2)}) async-start(bf16[4,64,8,128]{3,2,0,1:T(8,128)(2,1)} %copy.42), calls=%async_computation.1 | async-start | bytes 1048576 | tf_op jit(solution)/shard_map/all_to_all | solution.py:91
  68.8 23.4 %all-to-all-start = ((bf16[4,64,8,128]{3,2,0,1:T(8,128)(2,1)}), bf16[4,64,8,128]{3,2,0,1:T(8,128)(2,1)S(1)}, u32[]{:S(2)}, u32[]{:S(2)}) async-start(bf16[4,64,8,128]{3,2,0,1:T(8,128)(2,1)} %copy.40), calls=%async_computation | async-start | bytes 1048576 | tf_op jit(solution)/shard_map/all_to_all | solution.py:90
  74.5 115.8 %all-gather.2.cloned.1.call-start = ((), (), s32[]{:S(2)}) async-start(), calls=%async_computation.4 | async-start | bytes 4259840 | tf_op jit(solution)/shard_map/all_gather | solution.py:124
  94.9 15.1 %collective-permute-start = (bf16[2,4,512,128]{3,2,1,0:T(8,128)(2,1)S(1)}, bf16[2,4,512,128]{3,2,1,0:T(8,128)(2,1)S(1)}, u32[]{:S(2)}, u32[]{:S(2)}) collective-permute-start(bf16[2,4,512,128]{3,2,1,0:T(8,128)(2,1)S(1)} %pad_maximum_fusion.1), channel_id=1, source_target_pairs={{0,8},{8,16},{16,24},{24,32},{32,40},{40,48},{48,56},{56,64},{64,7... | collective-permute-start | bytes 3145736 | tf_op jit(solution)/shard_map/ppermute | solution.py:18
  98.3 16.2 %collective-permute-start.1 = (bf16[2,4,512,128]{3,2,1,0:T(8,128)(2,1)S(1)}, bf16[2,4,512,128]{3,2,1,0:T(8,128)(2,1)}, u32[]{:S(2)}, u32[]{:S(2)}) collective-permute-start(bf16[2,4,512,128]{3,2,1,0:T(8,128)(2,1)S(1)} %pad_maximum_fusion.1), channel_id=1, source_target_pairs={{8,0},{16,8},{24,16},{32,24},{40,32},{48,40},{56,48},{64,56},{72,6... | collective-permute-start | bytes 3145736 | tf_op jit(solution)/shard_map/ppermute | solution.py:20
  100.2 211.7 %all-reduce.3.cloned.1.call-start = ((), (), s32[]{:S(2)}) async-start(), calls=%async_computation.5 | async-start | bytes 8388608 | tf_op jit(solution)/shard_map/psum | solution.py:128
Sparse Core Ops, SparseCore 0:
  100.3 89.9 all-gather.1
  197.0 114.7 all-reduce.2
where the time goes:
time: 322 us; the launch traced here: 321 us
  waiting for transfers between devices  191 us (59%)
  blocking collectives  31.2 us (10%)
  starting transfers between devices  28.6 us (9%)
  local copies, waits for them, and re-layouts  23.8 us (7%)
  matrix products  21.4 us (7%)
  between operations  13.6 us (4%)
  other arithmetic  10.7 us (3%)
    psum x1, waiting for transfers between devices, shards(): lax.psum(partial_value.astype(jnp.bfloat16), 'tp').astype(jnp.float32)  115 us
    all_to_all x1, blocking collectives, shards(): lax.all_to_all(returning, 'seq', split_axis=1, concat_axis=1, tiled=True)  31.2 us
    all_to_all x1, waiting for transfers between devices, shards(): lax.all_to_all(outgoing(2), 'seq', split_axis=1, concat_axis=1, tiled=True)  16.8 us
    all_to_all x1, waiting for transfers between devices, shards(): lax.all_to_all(outgoing(1), 'seq', split_axis=1, concat_axis=1, tiled=True)  16.8 us
    all_to_all x1, waiting for transfers between devices, shards(): lax.all_to_all(outgoing(0), 'seq', split_axis=1, concat_axis=1, tiled=True)  16.1 us
    all_gather x1, waiting for transfers between devices, shards(): lax.all_gather(w_out, 'seq', axis=1, tiled=True)  11.8 us
    all_to_all x1, starting transfers between devices, shards(): lax.all_to_all(outgoing(2), 'seq', split_axis=1, concat_axis=1, tiled=True)  11.6 us
    ppermute x1, waiting for transfers between devices, extended_2(): lax.ppermute(tail, axis, [(i, (i + 1) % count) for i in range(ends)])  9.53 us
  transfers between devices with their start and end apart: 7, of which 7 were waited for; matrix products, arithmetic and copies ran while one was open for 11% of the time, Pallas kernels for 0%

commit v1 on v0

--- a/solution.py
+++ b/solution.py
@@ -5,6 +5,11 @@
 
 CLUSTER = 256
 REACH = 2
+
+
+def summed_here(x, name):
+    terms = lax.all_gather(x, name)
+    return jnp.sum(terms, axis=0)
 
 
 def extended_2(cells, sides, width):
@@ -125,7 +130,7 @@
         preferred_element_type=jnp.float32,
     )
     column_count = partial_value.shape[1] // lax.axis_size("tp")
-    summed = lax.psum(partial_value.astype(jnp.bfloat16), "tp").astype(jnp.float32)
+    summed = summed_here(partial_value.astype(jnp.bfloat16), "tp").astype(jnp.float32)
     mixed_out = lax.dynamic_slice_in_dim(
         summed, lax.axis_index("tp") * column_count, column_count, 1
     )

time: 322 us -> 554 us (1.72)
  waiting for transfers between devices: 191 us -> 409 us
  other arithmetic: 10.7 us -> 24.9 us
    all_gather x0 -> x1, waiting for transfers between devices: none -> 333 us  [summed_here(): terms = lax.all_gather(x, name)]
    psum x1 -> x0, waiting for transfers between devices: 115 us -> none  [shards(): lax.psum(partial_value.astype(jnp.bfloat16), 'tp').astype(jnp.float32)]
    reduce_sum x0 -> x1, other arithmetic: none -> 14.2 us  [summed_here(): return jnp.sum(terms, axis=0)]
  transfers between devices with their start and end apart: 7 -> 7, of which waited for: 7 -> 7; matrix products, arithmetic and copies ran while one was open for 11% -> 6% of each run, Pallas kernels for 0% -> 0%
where the time goes in v1:
time: 554 us; the launch traced here: 553 us
  waiting for transfers between devices  409 us (74%)
  blocking collectives  31.3 us (6%)
  starting transfers between devices  28.6 us (5%)
  other arithmetic  24.9 us (4%)
  local copies, waits for them, and re-layouts  23.7 us (4%)
  matrix products  21.4 us (4%)
  between operations  13.6 us (2%)
    all_gather x1, waiting for transfers between devices, summed_here(): terms = lax.all_gather(x, name)  333 us
    all_to_all x1, blocking collectives, shards(): lax.all_to_all(returning, 'seq', split_axis=1, concat_axis=1, tiled=True)  31.3 us
    all_to_all x1, waiting for transfers between devices, shards(): lax.all_to_all(outgoing(2), 'seq', split_axis=1, concat_axis=1, tiled=True)  16.8 us
    all_to_all x1, waiting for transfers between devices, shards(): lax.all_to_all(outgoing(1), 'seq', split_axis=1, concat_axis=1, tiled=True)  16.8 us
    all_to_all x1, waiting for transfers between devices, shards(): lax.all_to_all(outgoing(0), 'seq', split_axis=1, concat_axis=1, tiled=True)  16.1 us
    reduce_sum x1, other arithmetic, summed_here(): return jnp.sum(terms, axis=0)  14.2 us
    all_gather x1, waiting for transfers between devices, shards(): lax.all_gather(w_out, 'seq', axis=1, tiled=True)  11.7 us
    all_to_all x1, starting transfers between devices, shards(): lax.all_to_all(outgoing(2), 'seq', split_axis=1, concat_axis=1, tiled=True)  11.6 us
  transfers between devices with their start and end apart: 7, of which 7 were waited for; matrix products, arithmetic and copies ran while one was open for 6% of the time, Pallas kernels for 0%

profile of v1, /device:TPU:1, one launch (start us, length us, event | category | flops | bytes accessed | tf_op | source)
XLA Modules:
  0.0 552.9 jit_solution(14440029219832825550)
XLA Ops:
  6.5 0.8 add_select_fusion
  7.3 1.8 convert_reduce_fusion
  9.9 1.3 copy.34
  11.4 1.3 copy.35
  13.4 1.3 fusion.22
  15.0 0.9 copy.44
  15.9 11.6 %all-to-all-start.2 = ((bf16[4,64,8,128]{3,2,0,1:T(8,128)(2,1)}), bf16[4,64,8,128]{3,2,0,1:T(8,128)(2,1)S(1)}, u32[]{:S(2)}, u32[]{:S(2)}) async-start(bf16[4,64,8,128]{3,2,0,1:T(8,128)(2,1)} %copy.44), calls=%async_computation.2 | async-start | bytes 1048576 | tf_op jit(solution)/shard_map/all_to_all | solution.py:97
  27.5 0.9 copy.42
  28.4 16.8 %all-to-all-done.2 = bf16[4,64,8,128]{3,2,0,1:T(8,128)(2,1)S(1)} async-done(((bf16[4,64,8,128]{3,2,0,1:T(8,128)(2,1)}), bf16[4,64,8,128]{3,2,0,1:T(8,128)(2,1)S(1)}, u32[]{:S(2)}, u32[]{:S(2)}) %all-to-all-start.2) | async-done | bytes 524320 | tf_op jit(solution)/shard_map/all_to_all | solution.py:97
  45.2 5.7 %all-to-all-start.1 = ((bf16[4,64,8,128]{3,2,0,1:T(8,128)(2,1)}), bf16[4,64,8,128]{3,2,0,1:T(8,128)(2,1)S(1)}, u32[]{:S(2)}, u32[]{:S(2)}) async-start(bf16[4,64,8,128]{3,2,0,1:T(8,128)(2,1)} %copy.42), calls=%async_computation.1 | async-start | bytes 1048576 | tf_op jit(solution)/shard_map/all_to_all | solution.py:96
  51.0 0.9 copy.40
  51.8 16.8 %all-to-all-done.1 = bf16[4,64,8,128]{3,2,0,1:T(8,128)(2,1)S(1)} async-done(((bf16[4,64,8,128]{3,2,0,1:T(8,128)(2,1)}), bf16[4,64,8,128]{3,2,0,1:T(8,128)(2,1)S(1)}, u32[]{:S(2)}, u32[]{:S(2)}) %all-to-all-start.1) | async-done | bytes 524320 | tf_op jit(solution)/shard_map/all_to_all | solution.py:96
  68.7 5.7 %all-to-all-start = ((bf16[4,64,8,128]{3,2,0,1:T(8,128)(2,1)}), bf16[4,64,8,128]{3,2,0,1:T(8,128)(2,1)S(1)}, u32[]{:S(2)}, u32[]{:S(2)}) async-start(bf16[4,64,8,128]{3,2,0,1:T(8,128)(2,1)} %copy.40), calls=%async_computation | async-start | bytes 1048576 | tf_op jit(solution)/shard_map/all_to_all | solution.py:95
  74.6 1.2 convert_reduce_fusion.1
  76.0 16.1 %all-to-all-done = bf16[4,64,8,128]{3,2,0,1:T(8,128)(2,1)S(1)} async-done(((bf16[4,64,8,128]{3,2,0,1:T(8,128)(2,1)}), bf16[4,64,8,128]{3,2,0,1:T(8,128)(2,1)S(1)}, u32[]{:S(2)}, u32[]{:S(2)}) %all-to-all-start) | async-done | bytes 524320 | tf_op jit(solution)/shard_map/all_to_all | solution.py:95
  92.2 1.3 fusion.21
  93.5 1.2 slice_bitcast_fusion.3
  94.8 3.4 collective-permute-start
  98.2 1.9 collective-permute-start.1
  100.4 9.5 %collective-permute-done = bf16[2,4,512,128]{3,2,1,0:T(8,128)(2,1)S(1)} collective-permute-done((bf16[2,4,512,128]{3,2,1,0:T(8,128)(2,1)S(1)}, bf16[2,4,512,128]{3,2,1,0:T(8,128)(2,1)S(1)}, u32[]{:S(2)}, u32[]{:S(2)}) %collective-permute-start) | collective-permute-done | bytes 1048608 | tf_op jit(solution)/shard_map/ppermute | solution.py:23
  109.9 4.5 collective-permute-done.1
  114.4 1.3 pad_maximum_fusion
  115.7 1.4 slice_bitcast_fusion
  117.1 27.3 %while.16 = (s32[]{:T(128)}, bf16[4,512,128]{2,1,0:T(8,128)(2,1)}, s32[4,2,10]{2,1,0:T(2,128)}, bf16[4,512,128]{2,1,0:T(8,128)(2,1)}, bf16[4,1536,128]{2,1,0:T(8...) while((s32[]{:T(128)}, bf16[4,512,128]{2,1,0:T(8,128)(2,1)}, ...), condition=%wide.region_5.6_spmd, body=%wide.region_2.5_spmd.sunk | while | flops 509283360 | bytes 7096867 | solution.py:115
  117.1 1.1 dynamic-slice_bitcast_fusion.3
  118.7 0.9 constant_dynamic-slice_fusion.7
  120.4 1.0 fusion.65
  121.9 1.4 fusion.66
  124.0 1.0 dynamic-slice_bitcast_fusion.3
  125.5 0.9 constant_dynamic-slice_fusion.7
  127.2 1.0 fusion.65
  128.7 1.4 fusion.66
  130.8 1.0 dynamic-slice_bitcast_fusion.3
  132.3 0.9 constant_dynamic-slice_fusion.7
  134.0 1.0 fusion.65
  135.5 1.4 fusion.66
  137.6 1.1 dynamic-slice_bitcast_fusion.3
  139.1 0.9 constant_dynamic-slice_fusion.7
  140.8 1.0 fusion.65
  142.3 1.4 fusion.66
  144.4 1.8 fusion.35
  146.3 31.3 %all_to_all.20 = bf16[4,64,8,128]{3,2,0,1:T(8,128)(2,1)S(1)} all-to-all(bf16[4,64,8,128]{3,2,0,1:T(8,128)(2,1)S(1)} %copy.47), channel_id=1, replica_groups=mesh['seq'=64,'tp'=8] {'seq'}, dimensions={1} | all-to-all | bytes 1048576 | tf_op jit(solution)/shard_map/all_to_all | solution.py:120
  177.6 0.9 fusion.34
  178.5 11.7 %all-gather.4.cloned.1.call-done = bf16[512,4096]{0,1:T(8,128)(2,1)} async-done(((bf16[512,64]{0,1:T(8,128)(2,1)}), bf16[512,4096]{0,1:T(8,128)(2,1)}) %all-gather.4.cloned.1.call-update) | async-done | bytes 4194320 | tf_op jit(solution)/shard_map/all_gather | solution.py:129
  190.2 6.6 %convolution_convert_fusion = bf16[512,4096]{1,0:T(8,128)(2,1)} fusion(bf16[512,512]{0,1:T(8,128)(2,1)S(1)} %bitcast.114, bf16[512,4096]{0,1:T(8,128)(2,1)} %all-gather.4.cloned.1.call-done), kind=kOutput, calls=%fused_computation.26 | convolution fusion | flops 2149580800 | bytes 8912896 | tf_op jit(solution)/shard_map/dot_general | solution.py:127
  196.9 333.1 %all-gather.6.cloned.1.call-done = bf16[4096,4096]{1,0:T(8,128)(2,1)} async-done(((bf16[512,4096]{1,0:T(8,128)(2,1)}), bf16[4096,4096]{1,0:T(8,128)(2,1)}) %all-gather.6.cloned.1.call-update) | async-done | bytes 33554448 | tf_op jit(solution)/shard_map/all_gather | solution.py:11
  530.0 14.2 %reduce_sum.41 = bf16[512,4096]{1,0:T(8,128)(2,1)} reduce(bf16[8,512,4096]{2,1,0:T(8,128)(2,1)} %bitcast.100, bf16[]{:T(256)} %constant.60.clone.1), dimensions={0}, to_apply=%region_6.7 | reduce | flops 14680064 | bytes 37748736 | tf_op jit(solution)/shard_map/reduce_sum | solution.py:12
  544.2 1.9 convert_convert_fusion
  (95 shorter events, 15.3 us)
Async XLA Ops:
  6.5 6.4 %copy-start = (bf16[512,512]{1,0:T(8,128)(2,1)S(1)}, bf16[512,512]{1,0:T(8,128)(2,1)}, u32[]{:S(2)}) copy-start(bf16[512,512]{1,0:T(8,128)(2,1)} %param.11) | copy-start | bytes 1572868
  15.0 59.6 %copy-start.1 = (s32[4,512]{1,0:T(4,128)S(1)}, s32[4,512]{1,0:T(4,128)}, u32[]{:S(2)}) copy-start(s32[4,512]{1,0:T(4,128)} %param.13) | copy-start | bytes 24580
  15.9 29.3 %all-to-all-start.2 = ((bf16[4,64,8,128]{3,2,0,1:T(8,128)(2,1)}), bf16[4,64,8,128]{3,2,0,1:T(8,128)(2,1)S(1)}, u32[]{:S(2)}, u32[]{:S(2)}) async-start(bf16[4,64,8,128]{3,2,0,1:T(8,128)(2,1)} %copy.44), calls=%async_computation.2 | async-start | bytes 1048576 | tf_op jit(solution)/shard_map/all_to_all | solution.py:97
  45.2 23.4 %all-to-all-start.1 = ((bf16[4,64,8,128]{3,2,0,1:T(8,128)(2,1)}), bf16[4,64,8,128]{3,2,0,1:T(8,128)(2,1)S(1)}, u32[]{:S(2)}, u32[]{:S(2)}) async-start(bf16[4,64,8,128]{3,2,0,1:T(8,128)(2,1)} %copy.42), calls=%async_computation.1 | async-start | bytes 1048576 | tf_op jit(solution)/shard_map/all_to_all | solution.py:96
  68.7 23.4 %all-to-all-start = ((bf16[4,64,8,128]{3,2,0,1:T(8,128)(2,1)}), bf16[4,64,8,128]{3,2,0,1:T(8,128)(2,1)S(1)}, u32[]{:S(2)}, u32[]{:S(2)}) async-start(bf16[4,64,8,128]{3,2,0,1:T(8,128)(2,1)} %copy.40), calls=%async_computation | async-start | bytes 1048576 | tf_op jit(solution)/shard_map/all_to_all | solution.py:95
  74.4 115.8 %all-gather.4.cloned.1.call-start = ((), (), s32[]{:S(2)}) async-start(), calls=%async_computation.4 | async-start | bytes 4259840 | tf_op jit(solution)/shard_map/all_gather | solution.py:129
  94.8 15.1 %collective-permute-start = (bf16[2,4,512,128]{3,2,1,0:T(8,128)(2,1)S(1)}, bf16[2,4,512,128]{3,2,1,0:T(8,128)(2,1)S(1)}, u32[]{:S(2)}, u32[]{:S(2)}) collective-permute-start(bf16[2,4,512,128]{3,2,1,0:T(8,128)(2,1)S(1)} %pad_maximum_fusion.1), channel_id=1, source_target_pairs={{0,8},{8,16},{16,24},{24,32},{32,40},{40,48},{48,56},{56,64},{64,7... | collective-permute-start | bytes 3145736 | tf_op jit(solution)/shard_map/ppermute | solution.py:23
  98.2 16.2 %collective-permute-start.1 = (bf16[2,4,512,128]{3,2,1,0:T(8,128)(2,1)S(1)}, bf16[2,4,512,128]{3,2,1,0:T(8,128)(2,1)}, u32[]{:S(2)}, u32[]{:S(2)}) collective-permute-start(bf16[2,4,512,128]{3,2,1,0:T(8,128)(2,1)S(1)} %pad_maximum_fusion.1), channel_id=1, source_target_pairs={{8,0},{16,8},{24,16},{32,24},{40,32},{48,40},{56,48},{64,56},{72,6... | collective-permute-start | bytes 3145736 | tf_op jit(solution)/shard_map/ppermute | solution.py:25
  100.1 429.9 %all-gather.6.cloned.1.call-start = ((), (), s32[]{:S(2)}) async-start(), calls=%async_computation.5 | async-start | bytes 37748736 | tf_op jit(solution)/shard_map/all_gather | solution.py:11
Sparse Core Ops, SparseCore 0:
  100.2 89.9 all-gather.3
  197.0 332.9 all-gather.5
